TPU v7x, 32 devices: a whole 2x2x4 slice. The times are simulated.
32 devices in a mesh: groups: 2 (over x), seq: 16 (over z, y, core).
Axes of the slice: x: 2, y: 2, z: 4, core: 2. Of those that a mesh axis runs over, the one named last changes fastest.
Arguments:
- points: bfloat16 [32768, 1024], P(('groups', 'seq')), parts along dimension 0, may hold values from -110 to 110
- in_weight: bfloat16 [1024, 1536], P('seq'), may hold values from -0.1875 to 0.1875
- slice_token_weight: float32 [3, 64, 64], replicated, may hold values from -0.75 to 0.75
- cotangent: bfloat16 [32768, 1024], P(('groups', 'seq')), parts along dimension 0, may hold values from -48 to 48
Outputs:
- grad_points: bfloat16 [32768, 1024], P(('groups', 'seq')), parts along dimension 0
- grad_in_weight: float32 [2048, 1536], P(('groups', 'seq')), parts along dimension 0
- grad_token_weights: float32 [6, 64, 64], P('groups'), parts along dimension 0
There are 2 independent parts, one for each index of `groups`. A program takes and returns all parts, laid end to end along the dimension named above; an argument that names none is the same for every part. Nothing has to cross between parts.
All inputs are finite; a program needn't handle non-finite values.
Results may differ from a plain program's by a relative error of at most 0.012.
Values may be sent and summed in bfloat16 or wider, within the bound.
A program may use at most 128 MiB of HBM per device.

v0:
```python
import jax
import jax.numpy as jnp
from jax import lax
from jax.sharding import PartitionSpec as P

D = 1024
H = 16
M = 32
DH = 64


def token_mixing(slice_tokens, slice_token_weight):
    highest_precision = lax.Precision.HIGHEST
    query_rows = jnp.einsum(
        "pat,tg->pag", slice_tokens, slice_token_weight[0], precision=highest_precision
    )
    key_matrix = jnp.einsum(
        "pat,tg->pag", slice_tokens, slice_token_weight[1], precision=highest_precision
    )
    value_matrix = jnp.einsum(
        "pat,tg->pag", slice_tokens, slice_token_weight[2], precision=highest_precision
    )
    scores = jnp.einsum(
        "hme,hke->hmk", query_rows, key_matrix, precision=highest_precision
    ) / jnp.sqrt(jnp.float32(DH))
    attend = jax.nn.softmax(scores, axis=-1)
    return jnp.einsum("hmk,hke->hme", attend, value_matrix, precision=highest_precision)


def local(points, in_weight, slice_token_weight, cotangent):
    count = points.shape[0]
    whole_weight = lax.all_gather(in_weight, "seq", axis=0, tiled=True)
    projected = jnp.dot(points, whole_weight, preferred_element_type=jnp.float32)
    point_features = projected[:, :D].astype(jnp.bfloat16).reshape(count, H, DH)
    soft = jax.nn.softmax(projected[:, D:].reshape(count, H, M), axis=-1)
    backward_softmax = soft.astype(jnp.bfloat16)
    backward_gradient = cotangent.reshape(count, H, DH)
    mass = jnp.sum(backward_softmax.astype(jnp.float32), axis=0)
    slice_totals = jnp.einsum(
        "uog,uoa->oga", backward_softmax, point_features, preferred_element_type=jnp.float32
    )
    mass, slice_totals = lax.psum((mass, slice_totals), "seq")
    denom = mass + 1e-05
    slice_tokens = slice_totals / denom[:, :, None]
    mixed, mix_vjp = jax.vjp(token_mixing, slice_tokens, slice_token_weight)
    backward_mixed_tokens = mixed.astype(jnp.bfloat16)
    local_mixed_tokens = jnp.einsum(
        "uog,uoa->oga", backward_softmax, backward_gradient, preferred_element_type=jnp.float32
    )
    mixed_tokens_gradient = lax.psum(local_mixed_tokens, "seq")
    d_tokens, grad_token_weights = mix_vjp(mixed_tokens_gradient)
    slice_totals_gradient = (d_tokens / denom[:, :, None]).astype(jnp.bfloat16)
    slice_mass_gradient = -jnp.sum(d_tokens * slice_tokens, axis=-1) / denom
    softmax_gradient = jnp.einsum(
        "ugv,gfv->ugf", backward_gradient, backward_mixed_tokens, preferred_element_type=jnp.float32
    )
    softmax_gradient = (
        softmax_gradient
        + jnp.einsum(
            "ugv,gfv->ugf",
            point_features,
            slice_totals_gradient,
            preferred_element_type=jnp.float32,
        )
        + slice_mass_gradient[None]
    )
    d_logits = soft * (softmax_gradient - jnp.sum(soft * softmax_gradient, axis=-1, keepdims=True))
    feature_gradient = jnp.einsum(
        "lvt,vtz->lvz", backward_softmax, slice_totals_gradient, preferred_element_type=jnp.float32
    )
    grads = jnp.concatenate(
        [feature_gradient.reshape(count, D), d_logits.reshape(count, H * M)], axis=1
    ).astype(jnp.bfloat16)
    back = lax.dot_general(
        grads, whole_weight, (((1,), (1,)), ((), ())), preferred_element_type=jnp.float32
    )
    grad_points = back.astype(jnp.bfloat16)
    grad_in_weight = lax.psum_scatter(
        lax.dot_general(
            points, grads, (((0,), (0,)), ((), ())), preferred_element_type=jnp.float32
        ),
        "seq",
        scatter_dimension=0,
        tiled=True,
    )
    return (grad_points, grad_in_weight, grad_token_weights)


def solution(mesh):
    return jax.shard_map(
        local,
        mesh=mesh,
        in_specs=(P(("groups", "seq"), None), P("seq", None), P(), P(("groups", "seq"), None)),
        out_specs=(P(("groups", "seq"), None), P(("groups", "seq"), None), P("groups", None, None)),
        check_vma=False,
    )
```

profile of v0, /device:TPU:0, one launch (start us, length us, event | category | flops | bytes accessed | tf_op | source)
XLA Modules:
  0.0 333.9 jit_solution(10840951242688797717)
XLA Ops:
  8.0 4.0 %copy.27 = bf16[1024,1024]{0,1:T(8,128)(2,1)} copy(bf16[1024,1024]{1,0:T(8,128)(2,1)} %param.7) | data formatting | bytes 4194304 | tf_op args[3]
  11.9 46.3 %all-gather.2.cloned.1.call-done = bf16[1024,1536]{1,0:T(8,128)(2,1)} async-done(((bf16[64,1536]{1,0:T(8,128)(2,1)}), bf16[1024,1536]{1,0:T(8,128)(2,1)}) %all-gather.2.cloned.1.call-update) | async-done | bytes 3145744 | tf_op jit(solution)/shard_map/all_gather | solution.py:32
  58.2 5.3 %fusion.36 = f32[1024,1536]{1,0:T(8,128)S(1)} fusion(bf16[1024,1024]{1,0:T(8,128)(2,1)S(1)} %copy-done, bf16[1024,1536]{1,0:T(8,128)(2,1)} %all-gather.2.cloned.1.call-done), kind=kOutput, calls=%fused_computation.62 | convolution fusion | flops 3221225472 | bytes 11534336 | tf_op jit(solution)/shard_map/dot_general | solution.py:33
  63.5 1.8 slice.49
  65.3 1.5 copy-done.7
  66.8 1.5 slice.21
  68.3 3.9 %copy.24 = bf16[1024,1024]{0,1:T(8,128)(2,1)} copy(bf16[1024,1024]{1,0:T(8,128)(2,1)} %slice.49) | data formatting | bytes 4194304 | tf_op jit(solution)/shard_map/slice | solution.py:34
  72.2 2.9 copy.23
  75.1 2.0 bitcast_reduce_fusion
  78.3 1.0 copy-done.5
  79.3 1.4 fusion.38
  80.7 1.4 fusion.37
  82.2 1.6 div.58
  83.8 2.9 copy.26
  86.6 1.6 sub.29
  88.2 2.9 copy.25
  91.1 3.7 %convert_reduce_fusion = f32[512]{0:T(512)S(1)} fusion(f32[1024,512]{1,0:T(8,128)} %copy.26, f32[1024,512]{1,0:T(8,128)} %copy.25, f32[1024,1536]{1,0:T(8,128)} %copy-done.7), kind=kLoop, calls=%fused_computation.12 | loop fusion | flops 2620928 | bytes 6293504 | tf_op jit(solution)/shard_map/reduce_sum | solution.py:38
  94.9 32.0 %psum.22 = f32[16,32]{1,0:T(8,128)S(1)} all-reduce(f32[16,32]{1,0:T(8,128)S(1)} %reduce_sum.62), channel_id=1, replica_groups=mesh['groups'=2,'seq'=16] {'seq'}, use_global_device_ids=true, to_apply=%region_4.0 | all-reduce | flops 512 | bytes 4096 | tf_op jit(solution)/shard_map/psum | solution.py:42
  127.2 87.3 %all-reduce.6.cloned.1.call-done = (f32[16,32,64]{2,1,0:T(8,128)}, f32[16,32,64]{2,1,0:T(8,128)}) async-done(((f32[16,32,64]{2,1,0:T(8,128)}, f32[16,32,64]{2,1,0:T(8,128)}), (f32[16,32,64]{2,1,0:T(8,128)}, f32[16,32,64]{2,1,0:T(8,128)})) %all-reduce.6.cloned.1.call-update) | async-done | bytes 262160 | tf_op jit(solution)/shard_map/psum | solution.py:42
  214.4 1.4 fusion.20
  215.8 1.4 fusion.15
  217.3 1.4 fusion.23
  224.2 1.2 convolution_convert_fusion
  225.9 1.8 copy-done.2
  227.7 0.7 fusion.2
  228.4 6.4 %convolution_bitcast_fusion = f32[1024,1536]{0,1:T(8,128)} fusion(bf16[1024,1024]{1,0:T(8,128)(2,1)S(1)} %copy-done, bf16[1024,512]{0,1:T(8,128)(2,1)S(1)} %bitcast.102, bf16[1024,1024]{0,1:T(8,128)(2,1)S(1)} %bitcast.100), kind=kOutput, calls=%fused_computation.1 | convolution fusion | flops 3227516928 | bytes 11534336 | tf_op jit(solution)/shard_map/dot_general | solution.py:79
  234.9 6.6 %copy.33 = f32[1024,1536]{1,0:T(8,128)} copy(f32[1024,1536]{0,1:T(8,128)} %convolution_bitcast_fusion) | data formatting | bytes 12582912
  241.5 0.9 copy-done.13
  243.1 0.7 convolution_bitcast_fusion.1
  243.8 0.7 convolution_bitcast_fusion.3
  245.2 6.6 %fusion.5 = bf16[1024,1024]{1,0:T(8,128)(2,1)} fusion(bf16[1024,1536]{1,0:T(8,128)(2,1)} %all-gather.2.cloned.1.call-done, bf16[1024,512]{0,1:T(8,128)(2,1)S(1)} %bitcast.103, bf16[1024,1024]{0,1:T(8,128)(2,1)S(1)} %bitcast.101), kind=kOutput, calls=%fused_computation.16 | convolution fusion | flops 3228565504 | bytes 8388608 | tf_op jit(solution)/shard_map/dot_general | solution.py:74
  251.7 75.6 %reduce-scatter.4.cloned.1.call-done = f32[64,1536]{1,0:T(8,128)} async-done(((f32[1024,1536]{1,0:T(8,128)}), f32[64,1536]{1,0:T(8,128)}) %reduce-scatter.4.cloned.1.call-update) | async-done | bytes 393232
  (65 shorter events, 9.5 us)
Async XLA Ops:
  7.2 51.1 %copy-start = (bf16[1024,1024]{1,0:T(8,128)(2,1)S(1)}, bf16[1024,1024]{1,0:T(8,128)(2,1)}, u32[]{:S(2)}) copy-start(bf16[1024,1024]{1,0:T(8,128)(2,1)} %param.4) | copy-start | bytes 6291460
  7.2 51.0 %all-gather.2.cloned.1.call-start = ((), (), s32[]{:S(2)}) async-start(), calls=%async_computation.1 | async-start | bytes 3342336 | tf_op jit(solution)/shard_map/all_gather | solution.py:32
  7.9 206.5 %all-reduce.6.cloned.1.call-start = ((), (), s32[]{:S(2)}) async-start(), calls=%async_computation.3 | async-start | bytes 1048576 | tf_op jit(solution)/shard_map/psum | solution.py:42
  63.5 3.3 copy-start.7
  75.1 2.2 copy-start.1
  77.8 1.6 copy-start.5
  78.3 2.5 copy-start.3
  91.1 123.3 %copy-start.17 = (f32[3,64,64]{2,1,0:T(8,128)S(1)}, f32[3,64,64]{2,1,0:T(8,128)}, u32[]{:S(2)}) copy-start(f32[3,64,64]{2,1,0:T(8,128)} %param.6) | copy-start | bytes 147460
  126.9 200.4 %reduce-scatter.4.cloned.1.call-start = ((), (), s32[]{:S(2)}) async-start(), calls=%async_computation.2 | async-start | bytes 6684672
  215.8 4.1 %copy-start.16 = (f32[16,32,64]{2,1,0:T(8,128)S(1)}, f32[16,32,64]{2,1,0:T(8,128)}, u32[]{:S(2)}) copy-start(f32[16,32,64]{2,1,0:T(8,128)} %get-tuple-element.13) | copy-start | bytes 393220
  219.9 2.1 copy-start.6
  220.4 2.1 copy-start.10
  221.6 2.1 copy-start.14
  222.0 0.9 copy-start.18
  222.1 1.6 copy-start.12
  223.7 1.7 copy-start.4
  225.4 3.1 copy-start.8
  225.4 2.3 copy-start.2
  228.4 6.4 %copy-start.19 = (bf16[1024,16,32]{0,2,1:T(8,128)(2,1)}, bf16[1024,16,32]{0,2,1:T(8,128)(2,1)S(1)}, u32[]{:S(2)}) copy-start(bf16[1024,16,32]{0,2,1:T(8,128)(2,1)S(1)} %fusion.2) | copy-start | bytes 3145732
  241.4 0.9 copy-start.13
  241.4 1.7 copy-start.15
  241.4 2.4 copy-start.11
  242.4 2.8 copy-start.9
  242.4 2.8 copy-start.20
Sparse Core Ops, SparseCore 0:
  10.3 47.8 all-gather.1
  127.0 87.3 all-reduce.5
  241.6 85.7 reduce-scatter.3
where the time goes:
time: 335 us; the launch traced here: 334 us
  waiting for transfers between devices  210 us (63%)
  local copies, waits for them, and re-layouts  35.6 us (11%)
  matrix products  33.8 us (10%)
  blocking collectives  32 us (10%)
  between operations  14.1 us (4%)
  other arithmetic  8.17 us (2%)
    psum x1, waiting for transfers between devices, local(): mass, slice_totals = lax.psum((mass, slice_totals), 'seq')  87.3 us
    unnamed x4, waiting for transfers between devices  76.3 us
    all_gather x1, waiting for transfers between devices, local(): whole_weight = lax.all_gather(in_weight, 'seq', axis=0, tiled=True)  46.3 us
    psum x1, blocking collectives, local(): mass, slice_totals = lax.psum((mass, slice_totals), 'seq')  32 us
    unnamed x44, local copies, waits for them, and re-layouts  16.5 us
  transfers between devices with their start and end apart: 3, of which 3 were waited for; matrix products, arithmetic and copies ran while one was open for 4% of the time, Pallas kernels for 0%

commit v1 on v0

--- a/solution.py
+++ b/solution.py
@@ -1,6 +1,8 @@
 import jax
 import jax.numpy as jnp
 from jax import lax
+from jax.experimental import pallas as pl
+from jax.experimental.pallas import tpu as pltpu
 from jax.sharding import PartitionSpec as P
 
 D = 1024
@@ -86,9 +88,362 @@
     return (grad_points, grad_in_weight, grad_token_weights)
 
 
+MESH = pl.DeviceIdType.MESH
+F32 = jnp.float32
+BF16 = jnp.bfloat16
+HIGHEST = lax.Precision.HIGHEST
+N = 16
+Z = 4
+ROWS = D // N
+WIDTH = D + H * M
+
+
+def dot(a, b, dims=(1, 0), precision=None):
+    return lax.dot_general(
+        a, b, (((dims[0],), (dims[1],)), ((), ())), precision=precision, preferred_element_type=F32
+    )
+
+
+def kernel(
+    points, win, tw, cot, gp, gw, gtw,
+    w, pts_t, feat, soft, softb, stat, rbuf, full, dsum_m, mix_m, dmass, grads,
+    part, keep, cbuf, crbuf, ybuf, yrbuf, zbuf, zrbuf,
+    gsend, grecv, ssend, srecv, csend, crecv, ysend, yrecv, zsend, zrecv,
+):
+    count = points.shape[0]
+    tile = 256
+    me = lax.axis_index("seq")
+    z, y, c = me // 4, (me // 2) % 2, me % 2
+
+    def device(zz, yy, cc):
+        return (zz * 2 + yy) * 2 + cc
+
+    sibling, across = device(z, y, 1 - c), device(z, 1 - y, c)
+
+    def remote(src, dst, send, recv, to):
+        return pltpu.make_async_remote_copy(
+            src_ref=src, dst_ref=dst, send_sem=send, recv_sem=recv,
+            device_id={"seq": to}, device_id_type=MESH,
+        )
+
+    barrier = pltpu.get_barrier_semaphore()
+
+    @pl.loop(1, N)
+    def _(k):
+        pl.semaphore_signal(
+            barrier, inc=1, device_id={"seq": lax.rem(me + k, N)}, device_id_type=MESH
+        )
+
+    w[me] = win[...]
+    pl.semaphore_wait(barrier, N - 1)
+
+    def block(blk, slot, to):
+        return remote(w.at[blk], w.at[blk], gsend.at[slot, blk], grecv.at[blk], to)
+
+    up = jnp.minimum(z + 1, Z - 1)
+    down = jnp.maximum(z - 1, 0)
+    to_up, to_down = device(up, y, c), device(down, y, c)
+
+    def spread(blk):
+        block(blk, 2, across).start()
+        block(blk, 3, sibling).start()
+
+    @pl.when(z < Z - 1)
+    def _():
+        block(me, 0, to_up).start()
+
+    @pl.when(z > 0)
+    def _():
+        block(me, 1, to_down).start()
+
+    spread(me)
+
+    for k in range(D // tile):
+        cols = slice(k * tile, (k + 1) * tile)
+        pts_t[cols, :] = points[:, cols].T
+
+    for d in range(1, Z):
+        @pl.when(z - d >= 0)
+        def _():
+            blk = device(z - d, y, c)
+            block(blk, 0, to_up).wait_recv()
+
+            @pl.when(z < Z - 1)
+            def _():
+                block(blk, 0, to_up).start()
+
+            spread(blk)
+
+        @pl.when(z + d < Z)
+        def _():
+            blk = device(z + d, y, c)
+            block(blk, 1, to_down).wait_recv()
+
+            @pl.when(z > 0)
+            def _():
+                block(blk, 1, to_down).start()
+
+            spread(blk)
+
+    def relay(zz):
+        blk = device(zz, 1 - y, c)
+        block(blk, 2, across).wait_recv()
+        block(blk, 3, sibling).start()
+
+    relay(z)
+    for d in range(1, Z):
+        @pl.when(z - d >= 0)
+        def _():
+            relay(z - d)
+
+        @pl.when(z + d < Z)
+        def _():
+            relay(z + d)
+
+    for zz in range(Z):
+        for yy in range(2):
+            block(device(zz, yy, 1 - c), 3, sibling).wait_recv()
+
+    @pl.loop(0, count // tile)
+    def _(t):
+        rows = pl.ds(pl.multiple_of(t * tile, tile), tile)
+        projected = dot(points[rows, :], w[...].reshape(D, WIDTH))
+        feat[rows, :] = projected[:, :D].astype(BF16)
+        logits = projected[:, D:].T.reshape(H, M, tile)
+        e = jnp.exp(logits - jnp.max(logits, axis=1, keepdims=True))
+        s = (e / jnp.sum(e, axis=1, keepdims=True)).reshape(H * M, tile)
+        soft[:, rows] = s
+        softb[:, rows] = s.astype(BF16)
+
+    ones = jnp.ones((8, count), BF16)
+    for j in range(4):
+        sl, fl = slice(128 * j, 128 * j + 128), slice(256 * j, 256 * j + 256)
+        s = softb[sl, :]
+        rf, rg = dot(s, feat[:, fl]), dot(s, cot[:, fl])
+        mass = dot(ones, s, (1, 1))
+        for hh in range(4):
+            a, b = slice(32 * hh, 32 * hh + 32), slice(64 * hh, 64 * hh + 64)
+            stat[4 * j + hh, 0:32, :] = jnp.concatenate([rf[a, b], rg[a, b]], axis=1)
+            stat[4 * j + hh, 32:40, :] = mass
+
+    def piece(to):
+        return remote(stat.at[to], rbuf.at[me], ssend.at[0, to], srecv.at[0, me], to)
+
+    def landed(k):
+        return remote(stat.at[k], rbuf.at[k], ssend.at[0, k], srecv.at[0, k], k)
+
+    @pl.loop(1, N)
+    def _(k):
+        piece(lax.rem(me + k, N)).start()
+
+    rbuf[me] = stat[me]
+
+    @pl.loop(1, N)
+    def _(k):
+        landed(lax.rem(me + k, N)).wait_recv()
+
+    full[me] = jnp.sum(rbuf[...], axis=0)
+
+    def total(to):
+        return remote(full.at[me], full.at[me], ssend.at[1, to], srecv.at[1, me], to)
+
+    def total_landed(k):
+        return remote(full.at[k], full.at[k], ssend.at[1, k], srecv.at[1, k], k)
+
+    @pl.loop(1, N)
+    def _(k):
+        total(lax.rem(me + k, N)).start()
+
+    @pl.loop(1, N)
+    def _(k):
+        total_landed(lax.rem(me + k, N)).wait_recv()
+
+    wq, wk, wv = tw[0], tw[1], tw[2]
+    row_head = lax.broadcasted_iota(jnp.int32, (128, 128), 0) // M
+    col_head = lax.broadcasted_iota(jnp.int32, (128, 128), 1) // M
+    same = row_head == col_head
+    wide = (
+        lax.broadcasted_iota(jnp.int32, (128, 256), 0) // M
+        == lax.broadcasted_iota(jnp.int32, (128, 256), 1) // DH
+    )
+    gq = gk = gv = jnp.zeros((DH, DH), F32)
+    for j in range(4):
+        sums = full[4 * j : 4 * j + 4, 0:32, 0:64].reshape(128, DH)
+        d_mixed = full[4 * j : 4 * j + 4, 0:32, 64:128].reshape(128, DH)
+        denom = jnp.broadcast_to(full[4 * j, 32:33, :], (128, 128)).T[:, :DH] + 1e-05
+        tokens = sums / denom
+        q = dot(tokens, wq, precision=HIGHEST)
+        k = dot(tokens, wk, precision=HIGHEST)
+        v = dot(tokens, wv, precision=HIGHEST)
+        scores = dot(q, k, (1, 1), HIGHEST) * 0.125
+        scores = jnp.where(same, scores, -jnp.inf)
+        e = jnp.exp(scores - jnp.max(scores, axis=1, keepdims=True))
+        attend = e / jnp.sum(e, axis=1, keepdims=True)
+        mixed = dot(attend, v, precision=HIGHEST)
+        d_attend = dot(d_mixed, v, (1, 1), HIGHEST)
+        dv = dot(attend, d_mixed, (0, 0), HIGHEST)
+        d_attend = jnp.where(same, d_attend, 0.0)
+        ds = attend * (d_attend - jnp.sum(attend * d_attend, axis=1, keepdims=True)) * 0.125
+        dq = dot(ds, k, precision=HIGHEST)
+        dk = dot(ds, q, (0, 0), HIGHEST)
+        d_tokens = (
+            dot(dq, wq, (1, 1), HIGHEST)
+            + dot(dk, wk, (1, 1), HIGHEST)
+            + dot(dv, wv, (1, 1), HIGHEST)
+        )
+        gq += dot(tokens, dq, (0, 0), HIGHEST)
+        gk += dot(tokens, dk, (0, 0), HIGHEST)
+        gv += dot(tokens, dv, (0, 0), HIGHEST)
+        d_sums = d_tokens / denom
+        d_mass = -jnp.sum(d_tokens * tokens, axis=1, keepdims=True) / denom[:, 0:1]
+        sl = slice(128 * j, 128 * j + 128)
+        mix_m[sl, :] = jnp.where(wide, jnp.concatenate([mixed] * 4, axis=1), 0.0).astype(BF16)
+        dsum_m[sl, :] = jnp.where(wide, jnp.concatenate([d_sums] * 4, axis=1), 0.0).astype(BF16)
+        dmass[sl, :] = jnp.broadcast_to(d_mass, (128, 128))
+    gtw[0] = gq
+    gtw[1] = gk
+    gtw[2] = gv
+
+    for j in range(4):
+        sl, fl = slice(128 * j, 128 * j + 128), slice(256 * j, 256 * j + 256)
+        d_soft = (
+            dot(mix_m[sl, :], cot[:, fl], (1, 1))
+            + dot(dsum_m[sl, :], feat[:, fl], (1, 1))
+            + dmass[sl, 0:1]
+        )
+        s = soft[sl, :]
+        inner = jnp.sum((s * d_soft).reshape(4, M, count), axis=1, keepdims=True)
+        d_logits = s.reshape(4, M, count) * (d_soft.reshape(4, M, count) - inner)
+        grads[:, D + 128 * j : D + 128 * j + 128] = d_logits.reshape(128, count).T.astype(BF16)
+        grads[:, fl] = dot(softb[sl, :], dsum_m[sl, :], (0, 0)).astype(BF16)
+
+    def to_core(u):
+        return remote(cbuf.at[u], crbuf.at[u], csend.at[u], crecv.at[u], sibling)
+
+    def to_across(u):
+        return remote(ybuf.at[u], yrbuf.at[u], ysend.at[u], yrecv.at[u], across)
+
+    def to_owner(u):
+        return remote(
+            zbuf.at[u], zrbuf.at[u], zsend.at[u], zrecv.at[u],
+            device(lax.rem(z + 1 + u, Z), y, c),
+        )
+
+    unit = 4 * ROWS
+
+    @pl.loop(0, Z)
+    def _(u):
+        zz = lax.rem(z + 1 + u, Z)
+        rows = pl.ds(pl.multiple_of(zz * unit, unit), unit)
+        part[u] = dot(pts_t[rows, :], grads[...])
+        for yy in range(2):
+            other = pl.ds(pl.multiple_of(yy * 2 * ROWS + (1 - c) * ROWS, ROWS), ROWS)
+            cbuf[u, yy] = part[u, other, :].astype(BF16)
+        to_core(u).start()
+
+    @pl.loop(0, Z)
+    def _(u):
+        to_core(u).wait_recv()
+        theirs = pl.ds(pl.multiple_of((1 - y) * 2 * ROWS + c * ROWS, ROWS), ROWS)
+        mine = pl.ds(pl.multiple_of(y * 2 * ROWS + c * ROWS, ROWS), ROWS)
+        ybuf[u] = (part[u, theirs, :] + crbuf[u, 1 - y].astype(F32)).astype(BF16)
+        to_across(u).start()
+        keep[u] = part[u, mine, :] + crbuf[u, y].astype(F32)
+
+    @pl.loop(0, count // tile)
+    def _(t):
+        rows = pl.ds(pl.multiple_of(t * tile, tile), tile)
+        gp[rows, :] = dot(grads[rows, :], w[...].reshape(D, WIDTH), (1, 1)).astype(BF16)
+
+    @pl.loop(0, Z - 1)
+    def _(u):
+        to_across(u).wait_recv()
+        zbuf[u] = (keep[u] + yrbuf[u].astype(F32)).astype(BF16)
+        to_owner(u).start()
+
+    to_across(Z - 1).wait_recv()
+    own = keep[Z - 1] + yrbuf[Z - 1].astype(F32)
+    for u in range(Z - 1):
+        to_owner(u).wait_recv()
+        own = own + zrbuf[u].astype(F32)
+    gw[...] = own
+
+    for zz in range(Z):
+        block(device(zz, y, c), 2, across).wait_send()
+        for yy in range(2):
+            block(device(zz, yy, c), 3, sibling).wait_send()
+
+        @pl.when((z < Z - 1) & (zz <= z))
+        def _():
+            block(device(zz, y, c), 0, to_up).wait_send()
+
+        @pl.when((z > 0) & (zz >= z))
+        def _():
+            block(device(zz, y, c), 1, to_down).wait_send()
+
+    @pl.loop(1, N)
+    def _(k):
+        piece(lax.rem(me + k, N)).wait_send()
+        total(lax.rem(me + k, N)).wait_send()
+
+    @pl.loop(0, Z)
+    def _(u):
+        to_core(u).wait_send()
+        to_across(u).wait_send()
+
+    @pl.loop(0, Z - 1)
+    def _(u):
+        to_owner(u).wait_send()
+
+
+def fused(points, in_weight, slice_token_weight, cotangent):
+    count = points.shape[0]
+    vmem = pl.BlockSpec(memory_space=pltpu.VMEM)
+    dma = pltpu.SemaphoreType.DMA
+    return pl.pallas_call(
+        kernel,
+        out_shape=(
+            jax.ShapeDtypeStruct((count, D), BF16),
+            jax.ShapeDtypeStruct((ROWS, WIDTH), F32),
+            jax.ShapeDtypeStruct((3, DH, DH), F32),
+        ),
+        in_specs=[vmem] * 4,
+        out_specs=(vmem,) * 3,
+        scratch_shapes=[
+            pltpu.VMEM((N, ROWS, WIDTH), BF16),
+            pltpu.VMEM((D, count), BF16),
+            pltpu.VMEM((count, D), BF16),
+            pltpu.VMEM((H * M, count), F32),
+            pltpu.VMEM((H * M, count), BF16),
+            pltpu.VMEM((N, 40, 128), F32),
+            pltpu.VMEM((N, 40, 128), F32),
+            pltpu.VMEM((N, 40, 128), F32),
+            pltpu.VMEM((H * M, 256), BF16),
+            pltpu.VMEM((H * M, 256), BF16),
+            pltpu.VMEM((H * M, 128), F32),
+            pltpu.VMEM((count, WIDTH), BF16),
+            pltpu.VMEM((Z, 4 * ROWS, WIDTH), F32),
+            pltpu.VMEM((Z, ROWS, WIDTH), F32),
+            pltpu.VMEM((Z, 2, ROWS, WIDTH), BF16),
+            pltpu.VMEM((Z, 2, ROWS, WIDTH), BF16),
+            pltpu.VMEM((Z, ROWS, WIDTH), BF16),
+            pltpu.VMEM((Z, ROWS, WIDTH), BF16),
+            pltpu.VMEM((Z - 1, ROWS, WIDTH), BF16),
+            pltpu.VMEM((Z - 1, ROWS, WIDTH), BF16),
+            dma((4, N)), dma((N,)), dma((2, N)), dma((2, N)),
+            dma((Z,)), dma((Z,)), dma((Z,)), dma((Z,)), dma((Z - 1,)), dma((Z - 1,)),
+        ],
+        compiler_params=pltpu.CompilerParams(
+            collective_id=0, has_side_effects=True, vmem_limit_bytes=60 * 1024 * 1024
+        ),
+    )(points, in_weight, slice_token_weight, cotangent)
+
+
 def solution(mesh):
+    body = fused if mesh.shape["seq"] == N else local
+
     return jax.shard_map(
-        local,
+        body,
         mesh=mesh,
         in_specs=(P(("groups", "seq"), None), P("seq", None), P(), P(("groups", "seq"), None)),
         out_specs=(P(("groups", "seq"), None), P(("groups", "seq"), None), P("groups", None, None)),

time: 335 us -> 99.4 us (0.30)
  waiting for transfers between devices: 210 us -> 0 us
  Pallas kernels: 0 us -> 94 us
  matrix products: 33.8 us -> 0 us
  blocking collectives: 32 us -> 0 us
  local copies, waits for them, and re-layouts: 35.6 us -> 4.53 us
  between operations: 14.1 us -> 0.66 us
  other arithmetic: 8.17 us -> 0 us
    pallas_call x0 -> x1, Pallas kernels: none -> 94 us  [fused(): pl.pallas_call(kernel, out_shape=(jax.ShapeDtypeStruct((count, D), BF16),...]
    psum x1 -> x0, waiting for transfers between devices: 87.3 us -> none  [local(): mass, slice_totals = lax.psum((mass, slice_totals), 'seq')]
    unnamed x4 -> x0, waiting for transfers between devices: 76.3 us -> none
    all_gather x1 -> x0, waiting for transfers between devices: 46.3 us -> none  [local(): whole_weight = lax.all_gather(in_weight, 'seq', axis=0, tiled=True)]
    dot_general x23 -> x0, matrix products: 33.8 us -> none  [the longest x1 6.57 us: local(): lax.dot_general(grads, whole_weight, (((1,), (1,)), ((), ())), preferred_...]
    psum x1 -> x0, blocking collectives: 32 us -> none  [local(): mass, slice_totals = lax.psum((mass, slice_totals), 'seq')]
    unnamed x44 -> x7, local copies, waits for them, and re-layouts: 16.5 us -> 4.53 us
    slice x4 -> x0, local copies, waits for them, and re-layouts: 10.1 us -> none  [the longest x2 5.7 us: local(): point_features = projected[:, :D].astype(jnp.bfloat16).reshape(count, H, DH)]
  transfers between devices with their start and end apart: 3 -> 0, of which waited for: 3 -> 0; matrix products, arithmetic and copies ran while one was open for 4% -> 0% of each run, Pallas kernels for 0% -> 0%
where the time goes in v1:
time: 99.4 us; the launch traced here: 99.2 us
  Pallas kernels  94 us (95%)
  local copies, waits for them, and re-layouts  4.53 us (5%)
    pallas_call x1, Pallas kernels, fused(): pl.pallas_call(kernel, out_shape=(jax.ShapeDtypeStruct((count, D), BF16),...  94 us
    unnamed x7, local copies, waits for them, and re-layouts  4.53 us

profile of v1, /device:TPU:0, one launch (start us, length us, event | category | flops | bytes accessed | tf_op | source)
XLA Modules:
  0.0 99.2 jit_solution(16121797685087306753)
XLA Ops:
  0.6 94.0 %shard_map.67 = (bf16[1024,1024]{1,0:T(8,128)(2,1)}, f32[64,1536]{1,0:T(8,128)}, f32[3,64,64]{2,1,0:T(8,128)}) custom-call(bf16[1024,1024]{1,0:T(8,128)(2,1)} %points.1, bf16[64,1536]{1,0:T(8,128)(2,1)} %win.1, f32[3,64,64]{2,1,0:T(8,128)} %tw.1, bf16[1024,1024]{1,0:T(8,128)(2,1)} %cot.1), custom_call_target="tpu_custom_call" | custom-call | tf_op jit(solution)/shard_map/pallas_call | solution.py:403
  94.7 0.0 copy-start
  94.7 0.0 copy-start.1
  94.7 3.1 %copy.10 = bf16[1024,1024]{1,0:T(8,128)(2,1)} copy(bf16[1024,1024]{1,0:T(8,128)(2,1)} %get-tuple-element.6) | data formatting | bytes 4194304
  97.8 0.0 copy-done
  97.8 0.7 copy.11
  98.6 0.0 copy-done.1
  98.6 0.6 copy.12
Async XLA Ops:
  94.7 3.2 %copy-start = (f32[64,1536]{1,0:T(8,128)S(1)}, f32[64,1536]{1,0:T(8,128)}, u32[]{:S(2)}) copy-start(f32[64,1536]{1,0:T(8,128)} %get-tuple-element.7) | copy-start | bytes 1179652
  94.7 3.9 %copy-start.1 = (f32[3,64,64]{2,1,0:T(8,128)S(1)}, f32[3,64,64]{2,1,0:T(8,128)}, u32[]{:S(2)}) copy-start(f32[3,64,64]{2,1,0:T(8,128)} %get-tuple-element.8) | copy-start | bytes 147460

commit v2 on v1

--- a/solution.py
+++ b/solution.py
@@ -105,10 +105,10 @@
 
 
 def kernel(
-    points, win, tw, cot, gp, gw, gtw,
-    w, pts_t, feat, soft, softb, stat, rbuf, full, dsum_m, mix_m, dmass, grads,
+    points_hbm, win, tw, cot_hbm, gp_hbm, gw, gtw,
+    points, cot, gp, w, pts_t, feat, soft, softb, stat, rbuf, full, dsum_m, mix_m, dmass, grads,
     part, keep, cbuf, crbuf, ybuf, yrbuf, zbuf, zrbuf,
-    gsend, grecv, ssend, srecv, csend, crecv, ysend, yrecv, zsend, zrecv,
+    load, store, gsend, grecv, ssend, srecv, csend, crecv, ysend, yrecv, zsend, zrecv,
 ):
     count = points.shape[0]
     tile = 256
@@ -134,7 +134,14 @@
             barrier, inc=1, device_id={"seq": lax.rem(me + k, N)}, device_id_type=MESH
         )
 
-    w[me] = win[...]
+    loads = [
+        pltpu.make_async_copy(win, w.at[me], load.at[0]),
+        pltpu.make_async_copy(points_hbm, points, load.at[1]),
+        pltpu.make_async_copy(cot_hbm, cot, load.at[2]),
+    ]
+    for copy in loads:
+        copy.start()
+    loads[0].wait()
     pl.semaphore_wait(barrier, N - 1)
 
     def block(blk, slot, to):
@@ -158,11 +165,15 @@
 
     spread(me)
 
+    loads[1].wait()
     for k in range(D // tile):
         cols = slice(k * tile, (k + 1) * tile)
         pts_t[cols, :] = points[:, cols].T
 
-    for d in range(1, Z):
+    def partner(mask):
+        return 2 * lax.rem(z // 2 + mask // 2, 2) + lax.rem(z + mask, 2)
+
+    def forward(d):
         @pl.when(z - d >= 0)
         def _():
             blk = device(z - d, y, c)
@@ -185,29 +196,42 @@
 
             spread(blk)
 
-    def relay(zz):
+    def plane_arrives(zz):
         blk = device(zz, 1 - y, c)
         block(blk, 2, across).wait_recv()
         block(blk, 3, sibling).start()
-
-    relay(z)
-    for d in range(1, Z):
-        @pl.when(z - d >= 0)
-        def _():
-            relay(z - d)
-
-        @pl.when(z + d < Z)
-        def _():
-            relay(z + d)
-
-    for zz in range(Z):
         for yy in range(2):
             block(device(zz, yy, 1 - c), 3, sibling).wait_recv()
+
+    def plane_term(zz, rows):
+        cols = pl.ds(pl.multiple_of(zz * 4 * ROWS, 4 * ROWS), 4 * ROWS)
+        return dot(points[rows, cols], w[pl.ds(4 * zz, 4)].reshape(4 * ROWS, WIDTH))
+
+    @pl.loop(0, Z - 1)
+    def _(step):
+        forward(step + 1)
+        zz = partner(step)
+        plane_arrives(zz)
+
+        @pl.loop(0, count // tile)
+        def _(t):
+            term = plane_term(zz, pl.ds(pl.multiple_of(t * tile, tile), tile))
+
+            @pl.when(step == 0)
+            def _():
+                part[t] = term
+
+            @pl.when(step > 0)
+            def _():
+                part[t] += term
+
+    plane_arrives(partner(Z - 1))
+    loads[2].wait()
 
     @pl.loop(0, count // tile)
     def _(t):
         rows = pl.ds(pl.multiple_of(t * tile, tile), tile)
-        projected = dot(points[rows, :], w[...].reshape(D, WIDTH))
+        projected = part[t] + plane_term(partner(Z - 1), rows)
         feat[rows, :] = projected[:, :D].astype(BF16)
         logits = projected[:, D:].T.reshape(H, M, tile)
         e = jnp.exp(logits - jnp.max(logits, axis=1, keepdims=True))
@@ -323,26 +347,18 @@
     def to_across(u):
         return remote(ybuf.at[u], yrbuf.at[u], ysend.at[u], yrecv.at[u], across)
 
+    def unit_owner(u):
+        return partner(Z - 1 - u)
+
     def to_owner(u):
+        to = partner(2) if u == 1 else partner(1)
         return remote(
-            zbuf.at[u], zrbuf.at[u], zsend.at[u], zrecv.at[u],
-            device(lax.rem(z + 1 + u, Z), y, c),
+            zbuf.at[u], zrbuf.at[u], zsend.at[u], zrecv.at[u], device(to, y, c)
         )
 
     unit = 4 * ROWS
 
-    @pl.loop(0, Z)
-    def _(u):
-        zz = lax.rem(z + 1 + u, Z)
-        rows = pl.ds(pl.multiple_of(zz * unit, unit), unit)
-        part[u] = dot(pts_t[rows, :], grads[...])
-        for yy in range(2):
-            other = pl.ds(pl.multiple_of(yy * 2 * ROWS + (1 - c) * ROWS, ROWS), ROWS)
-            cbuf[u, yy] = part[u, other, :].astype(BF16)
-        to_core(u).start()
-
-    @pl.loop(0, Z)
-    def _(u):
+    def core_step(u):
         to_core(u).wait_recv()
         theirs = pl.ds(pl.multiple_of((1 - y) * 2 * ROWS + c * ROWS, ROWS), ROWS)
         mine = pl.ds(pl.multiple_of(y * 2 * ROWS + c * ROWS, ROWS), ROWS)
@@ -350,23 +366,56 @@
         to_across(u).start()
         keep[u] = part[u, mine, :] + crbuf[u, y].astype(F32)
 
-    @pl.loop(0, count // tile)
+    @pl.loop(0, Z)
+    def _(u):
+        rows = pl.ds(pl.multiple_of(unit_owner(u) * unit, unit), unit)
+        part[u] = dot(pts_t[rows, :], grads[...])
+        for yy in range(2):
+            other = pl.ds(pl.multiple_of(yy * 2 * ROWS + (1 - c) * ROWS, ROWS), ROWS)
+            cbuf[u, yy] = part[u, other, :].astype(BF16)
+        to_core(u).start()
+
+        @pl.when(u > 0)
+        def _():
+            core_step(u - 1)
+
+    core_step(Z - 1)
+
+    def gp_copy(t):
+        rows = pl.ds(pl.multiple_of(t * tile, tile), tile)
+        return pltpu.make_async_copy(gp.at[rows, :], gp_hbm.at[rows, :], store.at[t])
+
+    def gp_tiles(start, stop):
+        @pl.loop(start, stop)
+        def _(t):
+            rows = pl.ds(pl.multiple_of(t * tile, tile), tile)
+            gp[rows, :] = dot(grads[rows, :], w[...].reshape(D, WIDTH), (1, 1)).astype(BF16)
+            gp_copy(t).start()
+
+    def summed(u):
+        to_across(u).wait_recv()
+        return keep[u] + yrbuf[u].astype(F32)
+
+    tiles = count // tile
+    gp_tiles(0, tiles // 2)
+    zbuf[0] = summed(0).astype(BF16)
+    to_owner(0).start()
+    gp_tiles(tiles // 2, tiles)
+    second = summed(1)
+    to_owner(0).wait_recv()
+    zbuf[1] = (second + zrbuf[0].astype(F32)).astype(BF16)
+    to_owner(1).start()
+    zbuf[2] = summed(2).astype(BF16)
+    to_owner(2).start()
+    own = summed(3)
+    to_owner(1).wait_recv()
+    own = own + zrbuf[1].astype(F32)
+    to_owner(2).wait_recv()
+    gw[...] = own + zrbuf[2].astype(F32)
+
+    @pl.loop(0, tiles)
     def _(t):
-        rows = pl.ds(pl.multiple_of(t * tile, tile), tile)
-        gp[rows, :] = dot(grads[rows, :], w[...].reshape(D, WIDTH), (1, 1)).astype(BF16)
-
-    @pl.loop(0, Z - 1)
-    def _(u):
-        to_across(u).wait_recv()
-        zbuf[u] = (keep[u] + yrbuf[u].astype(F32)).astype(BF16)
-        to_owner(u).start()
-
-    to_across(Z - 1).wait_recv()
-    own = keep[Z - 1] + yrbuf[Z - 1].astype(F32)
-    for u in range(Z - 1):
-        to_owner(u).wait_recv()
-        own = own + zrbuf[u].astype(F32)
-    gw[...] = own
+        gp_copy(t).wait()
 
     for zz in range(Z):
         block(device(zz, y, c), 2, across).wait_send()
@@ -391,25 +440,48 @@
         to_core(u).wait_send()
         to_across(u).wait_send()
 
-    @pl.loop(0, Z - 1)
-    def _(u):
+    for u in range(Z - 1):
         to_owner(u).wait_send()
+
+
+def hand_on(*refs):
+    n = (len(refs) - 1) // 2
+    sems = refs[-1]
+    copies = []
+    for i in range(n):
+        src, dst = refs[i], refs[n + i]
+        pieces = 8 if i == 0 else 1
+        size = src.shape[0] // pieces
+        for k in range(pieces):
+            rows = pl.ds(k * size, size)
+            copies.append(
+                pltpu.make_async_copy(src.at[rows], dst.at[rows], sems.at[len(copies)])
+            )
+    for copy in copies:
+        copy.start()
+    for copy in copies:
+        copy.wait()
 
 
 def fused(points, in_weight, slice_token_weight, cotangent):
     count = points.shape[0]
     vmem = pl.BlockSpec(memory_space=pltpu.VMEM)
     dma = pltpu.SemaphoreType.DMA
-    return pl.pallas_call(
+    hbm = pl.BlockSpec(memory_space=pl.ANY)
+    out_shape = (
+        jax.ShapeDtypeStruct((count, D), BF16),
+        jax.ShapeDtypeStruct((ROWS, WIDTH), F32),
+        jax.ShapeDtypeStruct((3, DH, DH), F32),
+    )
+    outs = pl.pallas_call(
         kernel,
-        out_shape=(
-            jax.ShapeDtypeStruct((count, D), BF16),
-            jax.ShapeDtypeStruct((ROWS, WIDTH), F32),
-            jax.ShapeDtypeStruct((3, DH, DH), F32),
-        ),
-        in_specs=[vmem] * 4,
-        out_specs=(vmem,) * 3,
+        out_shape=out_shape,
+        in_specs=[hbm, hbm, vmem, hbm],
+        out_specs=(hbm, vmem, vmem),
         scratch_shapes=[
+            pltpu.VMEM((count, D), BF16),
+            pltpu.VMEM((count, D), BF16),
+            pltpu.VMEM((count, D), BF16),
             pltpu.VMEM((N, ROWS, WIDTH), BF16),
             pltpu.VMEM((D, count), BF16),
             pltpu.VMEM((count, D), BF16),
@@ -430,13 +502,20 @@
             pltpu.VMEM((Z, ROWS, WIDTH), BF16),
             pltpu.VMEM((Z - 1, ROWS, WIDTH), BF16),
             pltpu.VMEM((Z - 1, ROWS, WIDTH), BF16),
-            dma((4, N)), dma((N,)), dma((2, N)), dma((2, N)),
+            dma((3,)), dma((4,)), dma((4, N)), dma((N,)), dma((2, N)), dma((2, N)),
             dma((Z,)), dma((Z,)), dma((Z,)), dma((Z,)), dma((Z - 1,)), dma((Z - 1,)),
         ],
         compiler_params=pltpu.CompilerParams(
             collective_id=0, has_side_effects=True, vmem_limit_bytes=60 * 1024 * 1024
         ),
     )(points, in_weight, slice_token_weight, cotangent)
+    return pl.pallas_call(
+        hand_on,
+        out_shape=out_shape,
+        in_specs=[hbm] * 3,
+        out_specs=(hbm,) * 3,
+        scratch_shapes=[dma((10,))],
+    )(*outs)
 
 
 def solution(mesh):

time: 99.4 us -> 170 us (1.71)
  Pallas kernels: 94 us -> 170 us
  local copies, waits for them, and re-layouts: 4.53 us -> 0 us
    pallas_call x1 -> x2, Pallas kernels: 94 us -> 170 us  [the longest x1 90.1 us: fused(): pl.pallas_call(kernel, out_shape=out_shape, in_specs=[hbm, hbm, vmem, hbm...]
    unnamed x7 -> x0, local copies, waits for them, and re-layouts: 4.53 us -> none
where the time goes in v2:
time: 170 us
  Pallas kernels  170 us (100%)
    pallas_call x1, Pallas kernels, fused(): pl.pallas_call(kernel, out_shape=out_shape, in_specs=[hbm, hbm, vmem, hbm...  90.1 us
    pallas_call x1, Pallas kernels, fused(): pl.pallas_call(hand_on, out_shape=out_shape, in_specs=[hbm] * 3, out_spec...  79.6 us

profile of v2, /device:TPU:0, one launch (start us, length us, event | category | flops | bytes accessed | tf_op | source)
XLA Modules:
  0.0 170.3 jit_solution(14874187228318630428)
XLA Ops:
  0.6 90.1 %shard_map.67 = (bf16[1024,1024]{1,0:T(8,128)(2,1)}, f32[64,1536]{1,0:T(8,128)}, f32[3,64,64]{2,1,0:T(8,128)}) custom-call(bf16[1024,1024]{1,0:T(8,128)(2,1)} %points_hbm.1, bf16[64,1536]{1,0:T(8,128)(2,1)} %win.1, f32[3,64,64]{2,1,0:T(8,128)} %tw.1, bf16[1024,1024]{1,0:T(8,128)(2,1)} %cot_hbm.1), custom_call_target="tpu_custom_call" | custom-call | tf_op jit(solution)/shard_map/pallas_call | solution.py:476
  90.7 79.6 %shard_map.68 = (bf16[1024,1024]{1,0:T(8,128)(2,1)}, f32[64,1536]{1,0:T(8,128)}, f32[3,64,64]{2,1,0:T(8,128)}) custom-call(bf16[1024,1024]{1,0:T(8,128)(2,1)} %get-tuple-element.6.refs_0_, f32[64,1536]{1,0:T(8,128)} %get-tuple-element.7.refs_1_, f32[3,64,64]{2,1,0:T(8,128)} %get-tuple-element.8.refs_2_), custom_call_target="tpu_custom_call" | custom-call | tf_op jit(solution)/shard_map/pallas_call | solution.py:512

commit v3 on v2

--- a/solution.py
+++ b/solution.py
@@ -444,22 +444,21 @@
         to_owner(u).wait_send()
 
 
-def hand_on(*refs):
-    n = (len(refs) - 1) // 2
-    sems = refs[-1]
-    copies = []
-    for i in range(n):
-        src, dst = refs[i], refs[n + i]
-        pieces = 8 if i == 0 else 1
-        size = src.shape[0] // pieces
-        for k in range(pieces):
-            rows = pl.ds(k * size, size)
-            copies.append(
-                pltpu.make_async_copy(src.at[rows], dst.at[rows], sems.at[len(copies)])
-            )
-    for copy in copies:
+def hand_on(gp, gw, gtw, gp_out, gw_out, gtw_out, gp_v, gw_v, gtw_v, load, store):
+    size = gp.shape[0] // 4
+    steps = [
+        (gp.at[pl.ds(k * size, size)], gp_v.at[pl.ds(k * size, size)], gp_out.at[pl.ds(k * size, size)])
+        for k in range(4)
+    ]
+    steps += [(gw, gw_v, gw_out), (gtw, gtw_v, gtw_out)]
+    loads = [pltpu.make_async_copy(a, b, load.at[i]) for i, (a, b, _) in enumerate(steps)]
+    stores = [pltpu.make_async_copy(b, o, store.at[i]) for i, (_, b, o) in enumerate(steps)]
+    for copy in loads:
         copy.start()
-    for copy in copies:
+    for copy_in, copy_out in zip(loads, stores):
+        copy_in.wait()
+        copy_out.start()
+    for copy in stores:
         copy.wait()
 
 
@@ -514,7 +513,7 @@
         out_shape=out_shape,
         in_specs=[hbm] * 3,
         out_specs=(hbm,) * 3,
-        scratch_shapes=[dma((10,))],
+        scratch_shapes=[pltpu.VMEM(o.shape, o.dtype) for o in out_shape] + [dma((6,)), dma((6,))],
     )(*outs)
 
 

time: 170 us -> 93.5 us (0.55)
  Pallas kernels: 170 us -> 92.7 us
    pallas_call x1, Pallas kernels: 79.6 us -> 2.61 us  [fused(): pl.pallas_call(hand_on, out_shape=out_shape, in_specs=[hbm] * 3, out_spec...]
where the time goes in v3:
time: 93.5 us; the launch traced here: 93.3 us
  Pallas kernels  92.7 us (99%)
    pallas_call x1, Pallas kernels, fused(): pl.pallas_call(kernel, out_shape=out_shape, in_specs=[hbm, hbm, vmem, hbm...  90.1 us
    pallas_call x1, Pallas kernels, fused(): pl.pallas_call(hand_on, out_shape=out_shape, in_specs=[hbm] * 3, out_spec...  2.61 us

profile of v3, /device:TPU:0, one launch (start us, length us, event | category | flops | bytes accessed | tf_op | source)
XLA Modules:
  0.0 93.3 jit_solution(1063487354140656326)
XLA Ops:
  0.6 90.1 %shard_map.67 = (bf16[1024,1024]{1,0:T(8,128)(2,1)}, f32[64,1536]{1,0:T(8,128)}, f32[3,64,64]{2,1,0:T(8,128)}) custom-call(bf16[1024,1024]{1,0:T(8,128)(2,1)} %points_hbm.1, bf16[64,1536]{1,0:T(8,128)(2,1)} %win.1, f32[3,64,64]{2,1,0:T(8,128)} %tw.1, bf16[1024,1024]{1,0:T(8,128)(2,1)} %cot_hbm.1), custom_call_target="tpu_custom_call" | custom-call | tf_op jit(solution)/shard_map/pallas_call | solution.py:475
  90.7 2.6 %shard_map.68 = (bf16[1024,1024]{1,0:T(8,128)(2,1)}, f32[64,1536]{1,0:T(8,128)}, f32[3,64,64]{2,1,0:T(8,128)}) custom-call(bf16[1024,1024]{1,0:T(8,128)(2,1)} %get-tuple-element.6.gp, f32[64,1536]{1,0:T(8,128)} %get-tuple-element.7.gw, f32[3,64,64]{2,1,0:T(8,128)} %get-tuple-element.8.gtw), custom_call_target="tpu_custom_call" | custom-call | tf_op jit(solution)/shard_map/pallas_call | solution.py:511

commit v4 on v3

--- a/solution.py
+++ b/solution.py
@@ -107,7 +107,7 @@
 def kernel(
     points_hbm, win, tw, cot_hbm, gp_hbm, gw, gtw,
     points, cot, gp, w, pts_t, feat, soft, softb, stat, rbuf, full, dsum_m, mix_m, dmass, grads,
-    part, keep, cbuf, crbuf, ybuf, yrbuf, zbuf, zrbuf,
+    sbuf, part, keep, cbuf, crbuf, ybuf, yrbuf, zbuf, zrbuf,
     load, store, gsend, grecv, ssend, srecv, csend, crecv, ysend, yrecv, zsend, zrecv,
 ):
     count = points.shape[0]
@@ -247,40 +247,61 @@
         mass = dot(ones, s, (1, 1))
         for hh in range(4):
             a, b = slice(32 * hh, 32 * hh + 32), slice(64 * hh, 64 * hh + 64)
-            stat[4 * j + hh, 0:32, :] = jnp.concatenate([rf[a, b], rg[a, b]], axis=1)
-            stat[4 * j + hh, 32:40, :] = mass
-
-    def piece(to):
-        return remote(stat.at[to], rbuf.at[me], ssend.at[0, to], srecv.at[0, me], to)
+            stat[hh % 2, 2 * j + hh // 2, 0:32, :] = jnp.concatenate([rf[a, b], rg[a, b]], axis=1)
+            stat[hh % 2, 2 * j + hh // 2, 32:40, :] = mass
+
+    half = N // 2
+    q = me // 2
+    halves = remote(stat.at[1 - c], sbuf, ssend.at[0, q], srecv.at[0, q], sibling)
+    halves.start()
+    halves.wait_recv()
+
+    @pl.loop(0, half)
+    def _(k):
+        stat[c, k] += sbuf[k]
+
+    def peer(k):
+        return lax.rem(q + k, half)
+
+    def piece(k):
+        return remote(
+            stat.at[c, k], rbuf.at[q], ssend.at[0, k], srecv.at[0, q], 2 * k + c
+        )
 
     def landed(k):
-        return remote(stat.at[k], rbuf.at[k], ssend.at[0, k], srecv.at[0, k], k)
-
-    @pl.loop(1, N)
-    def _(k):
-        piece(lax.rem(me + k, N)).start()
-
-    rbuf[me] = stat[me]
-
-    @pl.loop(1, N)
-    def _(k):
-        landed(lax.rem(me + k, N)).wait_recv()
-
-    full[me] = jnp.sum(rbuf[...], axis=0)
-
-    def total(to):
-        return remote(full.at[me], full.at[me], ssend.at[1, to], srecv.at[1, me], to)
+        return remote(stat.at[c, k], rbuf.at[k], ssend.at[0, k], srecv.at[0, k], 2 * k + c)
+
+    @pl.loop(1, half)
+    def _(k):
+        piece(peer(k)).start()
+
+    rbuf[q] = stat[c, q]
+
+    @pl.loop(1, half)
+    def _(k):
+        landed(peer(k)).wait_recv()
+
+    full[c, q] = jnp.sum(rbuf[...], axis=0)
+
+    def total(k):
+        return remote(
+            full.at[c, q], full.at[c, q], ssend.at[1, k], srecv.at[1, q], 2 * k + c
+        )
 
     def total_landed(k):
-        return remote(full.at[k], full.at[k], ssend.at[1, k], srecv.at[1, k], k)
-
-    @pl.loop(1, N)
-    def _(k):
-        total(lax.rem(me + k, N)).start()
-
-    @pl.loop(1, N)
-    def _(k):
-        total_landed(lax.rem(me + k, N)).wait_recv()
+        return remote(full.at[c, k], full.at[c, k], ssend.at[1, k], srecv.at[1, k], 2 * k + c)
+
+    @pl.loop(1, half)
+    def _(k):
+        total(peer(k)).start()
+
+    @pl.loop(1, half)
+    def _(k):
+        total_landed(peer(k)).wait_recv()
+
+    whole = remote(full.at[c], full.at[c], ssend.at[1, q], srecv.at[1, q], sibling)
+    whole.start()
+    whole.wait_recv()
 
     wq, wk, wv = tw[0], tw[1], tw[2]
     row_head = lax.broadcasted_iota(jnp.int32, (128, 128), 0) // M
@@ -290,40 +311,63 @@
         lax.broadcasted_iota(jnp.int32, (128, 256), 0) // M
         == lax.broadcasted_iota(jnp.int32, (128, 256), 1) // DH
     )
-    gq = gk = gv = jnp.zeros((DH, DH), F32)
-    for j in range(4):
-        sums = full[4 * j : 4 * j + 4, 0:32, 0:64].reshape(128, DH)
-        d_mixed = full[4 * j : 4 * j + 4, 0:32, 64:128].reshape(128, DH)
-        denom = jnp.broadcast_to(full[4 * j, 32:33, :], (128, 128)).T[:, :DH] + 1e-05
-        tokens = sums / denom
-        q = dot(tokens, wq, precision=HIGHEST)
-        k = dot(tokens, wk, precision=HIGHEST)
-        v = dot(tokens, wv, precision=HIGHEST)
-        scores = dot(q, k, (1, 1), HIGHEST) * 0.125
-        scores = jnp.where(same, scores, -jnp.inf)
-        e = jnp.exp(scores - jnp.max(scores, axis=1, keepdims=True))
-        attend = e / jnp.sum(e, axis=1, keepdims=True)
-        mixed = dot(attend, v, precision=HIGHEST)
-        d_attend = dot(d_mixed, v, (1, 1), HIGHEST)
-        dv = dot(attend, d_mixed, (0, 0), HIGHEST)
-        d_attend = jnp.where(same, d_attend, 0.0)
-        ds = attend * (d_attend - jnp.sum(attend * d_attend, axis=1, keepdims=True)) * 0.125
-        dq = dot(ds, k, precision=HIGHEST)
-        dk = dot(ds, q, (0, 0), HIGHEST)
-        d_tokens = (
-            dot(dq, wq, (1, 1), HIGHEST)
-            + dot(dk, wk, (1, 1), HIGHEST)
-            + dot(dv, wv, (1, 1), HIGHEST)
-        )
-        gq += dot(tokens, dq, (0, 0), HIGHEST)
-        gk += dot(tokens, dk, (0, 0), HIGHEST)
-        gv += dot(tokens, dv, (0, 0), HIGHEST)
-        d_sums = d_tokens / denom
-        d_mass = -jnp.sum(d_tokens * tokens, axis=1, keepdims=True) / denom[:, 0:1]
+    groups = range(4)
+
+    def heads_of(j, rows, lanes):
+        return [full[hh % 2, 2 * j + hh // 2, rows, lanes] for hh in range(4)]
+
+    def cut(x):
+        return [x[128 * j : 128 * j + 128] for j in groups]
+
+    def join(parts):
+        return jnp.concatenate(parts, axis=0)
+
+    def each(a, b, dims):
+        return [dot(a[j], b[j], dims, HIGHEST) for j in groups]
+
+    lanes_a, lanes_b = slice(0, DH), slice(DH, 2 * DH)
+    sums = join([join(heads_of(j, slice(0, 32), lanes_a)) for j in groups])
+    d_mixed = [join(heads_of(j, slice(0, 32), lanes_b)) for j in groups]
+    denom = (
+        join(
+            [jnp.broadcast_to(full[0, 2 * j, 32:33, :], (128, 128)).T[:, :DH] for j in groups]
+        )
+        + 1e-05
+    )
+    tokens = sums / denom
+    q_rows = cut(dot(tokens, wq, precision=HIGHEST))
+    k_rows = cut(dot(tokens, wk, precision=HIGHEST))
+    v_rows = cut(dot(tokens, wv, precision=HIGHEST))
+    scores = each(q_rows, k_rows, (1, 1))
+    d_attend = each(d_mixed, v_rows, (1, 1))
+    attend = []
+    for j in groups:
+        shown = jnp.where(same, scores[j] * 0.125, -jnp.inf)
+        e = jnp.exp(shown - jnp.max(shown, axis=1, keepdims=True))
+        attend.append(e / jnp.sum(e, axis=1, keepdims=True))
+    ds = []
+    for j in groups:
+        da = jnp.where(same, d_attend[j], 0.0)
+        ds.append(attend[j] * (da - jnp.sum(attend[j] * da, axis=1, keepdims=True)) * 0.125)
+    dq = join(each(ds, k_rows, (1, 0)))
+    dk = join(each([x.T for x in ds], q_rows, (1, 0)))
+    dv = join(each([x.T for x in attend], d_mixed, (1, 0)))
+    mixed = each(attend, v_rows, (1, 0))
+    d_tokens = (
+        dot(dq, wq, (1, 1), HIGHEST)
+        + dot(dk, wk, (1, 1), HIGHEST)
+        + dot(dv, wv, (1, 1), HIGHEST)
+    )
+    d_sums = cut(d_tokens / denom)
+    d_mass = cut(-jnp.sum(d_tokens * tokens, axis=1, keepdims=True) / denom[:, 0:1])
+    for j in groups:
         sl = slice(128 * j, 128 * j + 128)
-        mix_m[sl, :] = jnp.where(wide, jnp.concatenate([mixed] * 4, axis=1), 0.0).astype(BF16)
-        dsum_m[sl, :] = jnp.where(wide, jnp.concatenate([d_sums] * 4, axis=1), 0.0).astype(BF16)
-        dmass[sl, :] = jnp.broadcast_to(d_mass, (128, 128))
+        mix_m[sl, :] = jnp.where(wide, jnp.concatenate([mixed[j]] * 4, axis=1), 0.0).astype(BF16)
+        dsum_m[sl, :] = jnp.where(wide, jnp.concatenate([d_sums[j]] * 4, axis=1), 0.0).astype(BF16)
+        dmass[sl, :] = jnp.broadcast_to(d_mass[j], (128, 128))
+    gq = dot(tokens, dq, (0, 0), HIGHEST)
+    gk = dot(tokens, dk, (0, 0), HIGHEST)
+    gv = dot(tokens, dv, (0, 0), HIGHEST)
     gtw[0] = gq
     gtw[1] = gk
     gtw[2] = gv
@@ -430,10 +474,13 @@
         def _():
             block(device(zz, y, c), 1, to_down).wait_send()
 
-    @pl.loop(1, N)
-    def _(k):
-        piece(lax.rem(me + k, N)).wait_send()
-        total(lax.rem(me + k, N)).wait_send()
+    @pl.loop(1, N // 2)
+    def _(k):
+        piece(peer(k)).wait_send()
+        total(peer(k)).wait_send()
+
+    halves.wait_send()
+    whole.wait_send()
 
     @pl.loop(0, Z)
     def _(u):
@@ -486,13 +533,14 @@
             pltpu.VMEM((count, D), BF16),
             pltpu.VMEM((H * M, count), F32),
             pltpu.VMEM((H * M, count), BF16),
-            pltpu.VMEM((N, 40, 128), F32),
-            pltpu.VMEM((N, 40, 128), F32),
-            pltpu.VMEM((N, 40, 128), F32),
+            pltpu.VMEM((2, N // 2, 40, 128), F32),
+            pltpu.VMEM((N // 2, 40, 128), F32),
+            pltpu.VMEM((2, N // 2, 40, 128), F32),
             pltpu.VMEM((H * M, 256), BF16),
             pltpu.VMEM((H * M, 256), BF16),
             pltpu.VMEM((H * M, 128), F32),
             pltpu.VMEM((count, WIDTH), BF16),
+            pltpu.VMEM((N // 2, 40, 128), F32),
             pltpu.VMEM((Z, 4 * ROWS, WIDTH), F32),
             pltpu.VMEM((Z, ROWS, WIDTH), F32),
             pltpu.VMEM((Z, 2, ROWS, WIDTH), BF16),

time: 93.5 us -> 85.2 us (0.911)
  Pallas kernels: 92.7 us -> 84.4 us
    pallas_call x1, Pallas kernels: 90.1 us -> 81.8 us  [fused(): pl.pallas_call(kernel, out_shape=out_shape, in_specs=[hbm, hbm, vmem, hbm...]
where the time goes in v4:
time: 85.2 us; the launch traced here: 85 us
  Pallas kernels  84.4 us (99%)
    pallas_call x1, Pallas kernels, fused(): pl.pallas_call(kernel, out_shape=out_shape, in_specs=[hbm, hbm, vmem, hbm...  81.8 us
    pallas_call x1, Pallas kernels, fused(): pl.pallas_call(hand_on, out_shape=out_shape, in_specs=[hbm] * 3, out_spec...  2.61 us

profile of v4, /device:TPU:0, one launch (start us, length us, event | category | flops | bytes accessed | tf_op | source)
XLA Modules:
  0.0 85.0 jit_solution(5433155704168614538)
XLA Ops:
  0.6 81.8 %shard_map.67 = (bf16[1024,1024]{1,0:T(8,128)(2,1)}, f32[64,1536]{1,0:T(8,128)}, f32[3,64,64]{2,1,0:T(8,128)}) custom-call(bf16[1024,1024]{1,0:T(8,128)(2,1)} %points_hbm.1, bf16[64,1536]{1,0:T(8,128)(2,1)} %win.1, f32[3,64,64]{2,1,0:T(8,128)} %tw.1, bf16[1024,1024]{1,0:T(8,128)(2,1)} %cot_hbm.1), custom_call_target="tpu_custom_call" | custom-call | tf_op jit(solution)/shard_map/pallas_call | solution.py:522
  82.4 2.6 %shard_map.68 = (bf16[1024,1024]{1,0:T(8,128)(2,1)}, f32[64,1536]{1,0:T(8,128)}, f32[3,64,64]{2,1,0:T(8,128)}) custom-call(bf16[1024,1024]{1,0:T(8,128)(2,1)} %get-tuple-element.6.gp, f32[64,1536]{1,0:T(8,128)} %get-tuple-element.7.gw, f32[3,64,64]{2,1,0:T(8,128)} %get-tuple-element.8.gtw), custom_call_target="tpu_custom_call" | custom-call | tf_op jit(solution)/shard_map/pallas_call | solution.py:559

commit v5 on v4

--- a/solution.py
+++ b/solution.py
@@ -134,6 +134,10 @@
             barrier, inc=1, device_id={"seq": lax.rem(me + k, N)}, device_id_type=MESH
         )
 
+    g = lax.axis_index("groups")
+    twin = {"groups": 1 - g, "seq": me}
+    pl.semaphore_signal(barrier, inc=1, device_id=twin, device_id_type=MESH)
+
     loads = [
         pltpu.make_async_copy(win, w.at[me], load.at[0]),
         pltpu.make_async_copy(points_hbm, points, load.at[1]),
@@ -142,7 +146,7 @@
     for copy in loads:
         copy.start()
     loads[0].wait()
-    pl.semaphore_wait(barrier, N - 1)
+    pl.semaphore_wait(barrier, N)
 
     def block(blk, slot, to):
         return remote(w.at[blk], w.at[blk], gsend.at[slot, blk], grecv.at[blk], to)
@@ -151,8 +155,20 @@
     down = jnp.maximum(z - 1, 0)
     to_up, to_down = device(up, y, c), device(down, y, c)
 
+    def over_y(zz):
+        return lax.rem(zz, 2) == g
+
+    def to_twin(blk):
+        return pltpu.make_async_remote_copy(
+            src_ref=w.at[blk], dst_ref=w.at[blk], send_sem=gsend.at[4, blk],
+            recv_sem=grecv.at[blk], device_id=twin, device_id_type=MESH,
+        )
+
     def spread(blk):
-        block(blk, 2, across).start()
+        @pl.when(over_y(blk // 4))
+        def _():
+            block(blk, 2, across).start()
+
         block(blk, 3, sibling).start()
 
     @pl.when(z < Z - 1)
@@ -199,6 +215,11 @@
     def plane_arrives(zz):
         blk = device(zz, 1 - y, c)
         block(blk, 2, across).wait_recv()
+
+        @pl.when(over_y(zz))
+        def _():
+            to_twin(blk).start()
+
         block(blk, 3, sibling).start()
         for yy in range(2):
             block(device(zz, yy, 1 - c), 3, sibling).wait_recv()
@@ -462,7 +483,11 @@
         gp_copy(t).wait()
 
     for zz in range(Z):
-        block(device(zz, y, c), 2, across).wait_send()
+        @pl.when(over_y(zz))
+        def _():
+            block(device(zz, y, c), 2, across).wait_send()
+            to_twin(device(zz, 1 - y, c)).wait_send()
+
         for yy in range(2):
             block(device(zz, yy, c), 3, sibling).wait_send()
 
@@ -549,7 +574,7 @@
             pltpu.VMEM((Z, ROWS, WIDTH), BF16),
             pltpu.VMEM((Z - 1, ROWS, WIDTH), BF16),
             pltpu.VMEM((Z - 1, ROWS, WIDTH), BF16),
-            dma((3,)), dma((4,)), dma((4, N)), dma((N,)), dma((2, N)), dma((2, N)),
+            dma((3,)), dma((4,)), dma((5, N)), dma((N,)), dma((2, N)), dma((2, N)),
             dma((Z,)), dma((Z,)), dma((Z,)), dma((Z,)), dma((Z - 1,)), dma((Z - 1,)),
         ],
         compiler_params=pltpu.CompilerParams(
@@ -566,7 +591,7 @@
 
 
 def solution(mesh):
-    body = fused if mesh.shape["seq"] == N else local
+    body = fused if mesh.shape["seq"] == N and mesh.shape["groups"] == 2 else local
 
     return jax.shard_map(
         body,

time: 85.2 us -> 100 us (1.17)
  Pallas kernels: 84.4 us -> 99.3 us
    pallas_call x1, Pallas kernels: 81.8 us -> 96.7 us  [fused(): pl.pallas_call(kernel, out_shape=out_shape, in_specs=[hbm, hbm, vmem, hbm...]
where the time goes in v5:
time: 100 us; the launch traced here: 99.9 us
  Pallas kernels  99.3 us (99%)
    pallas_call x1, Pallas kernels, fused(): pl.pallas_call(kernel, out_shape=out_shape, in_specs=[hbm, hbm, vmem, hbm...  96.7 us
    pallas_call x1, Pallas kernels, fused(): pl.pallas_call(hand_on, out_shape=out_shape, in_specs=[hbm] * 3, out_spec...  2.61 us

profile of v5, /device:TPU:0, one launch (start us, length us, event | category | flops | bytes accessed | tf_op | source)
XLA Modules:
  0.0 99.9 jit_solution(9242943416210464631)
XLA Ops:
  0.6 96.7 %shard_map.67 = (bf16[1024,1024]{1,0:T(8,128)(2,1)}, f32[64,1536]{1,0:T(8,128)}, f32[3,64,64]{2,1,0:T(8,128)}) custom-call(bf16[1024,1024]{1,0:T(8,128)(2,1)} %points_hbm.1, bf16[64,1536]{1,0:T(8,128)(2,1)} %win.1, f32[3,64,64]{2,1,0:T(8,128)} %tw.1, bf16[1024,1024]{1,0:T(8,128)(2,1)} %cot_hbm.1), custom_call_target="tpu_custom_call" | custom-call | tf_op jit(solution)/shard_map/pallas_call | solution.py:547
  97.3 2.6 %shard_map.68 = (bf16[1024,1024]{1,0:T(8,128)(2,1)}, f32[64,1536]{1,0:T(8,128)}, f32[3,64,64]{2,1,0:T(8,128)}) custom-call(bf16[1024,1024]{1,0:T(8,128)(2,1)} %get-tuple-element.6.gp, f32[64,1536]{1,0:T(8,128)} %get-tuple-element.7.gw, f32[3,64,64]{2,1,0:T(8,128)} %get-tuple-element.8.gtw), custom_call_target="tpu_custom_call" | custom-call | tf_op jit(solution)/shard_map/pallas_call | solution.py:584
